TPU v7x, 32 devices: a whole 2x2x4 slice. The times are simulated.
32 devices in a mesh: ep: 8 (over z, y), tp: 4 (over x, core).
Axes of the slice: x: 2, y: 2, z: 4, core: 2. Of those that a mesh axis runs over, the one named last changes fastest.
Arguments:
- tokens: bfloat16 [4096, 1536], P(('ep', 'tp')), may hold values from -6 to 6
- norm_gain: float32 [1536], replicated, may hold values from 0.5 to 1.5
- query_matrix: bfloat16 [1536, 1536], P(None, 'tp'), may hold values from -0.15625 to 0.15625
- key_matrix: bfloat16 [1536, 512], P(None, 'tp'), may hold values from -0.15625 to 0.15625
- value_matrix: bfloat16 [1536, 512], P(None, 'tp'), may hold values from -0.15625 to 0.15625
- out_weight: bfloat16 [1536, 1536], P('tp'), may hold values from -1.25 to 1.25
- moe_gain: float32 [1536], replicated, may hold values from 0.5 to 1.5
- router_weight: bfloat16 [1536, 40], replicated, may hold values from -0.0390625 to 0.0390625
- gate_weight: bfloat16 [40, 1536, 512], P('ep', None, 'tp'), may hold values from -0.15625 to 0.15625
- up_weight: bfloat16 [40, 1536, 512], P('ep', None, 'tp'), may hold values from -0.15625 to 0.15625
- down_weight: bfloat16 [40, 512, 1536], P('ep', 'tp'), may hold values from -2 to 2
- cotangent: bfloat16 [4096, 1536], P(('ep', 'tp')), may hold values from -6 to 6
- expert_ids: int32 [4096, 8], P(('ep', 'tp')), may hold values from 0 to 39, all different within a row; in each aligned block of 128 rows (0 to 127, 128 to 255, ...) at most 32 rows name the same one
- segments: int32 [8, 512], P('ep'), may hold values from 0 to 3, never falling along the last dimension, each value on 1 to 256 neighbouring positions
- valid_mask: int32 [8, 512], P('ep'), may hold values from 0 to 1, as said below
Outputs:
- output: bfloat16 [4096, 1536], P(('ep', 'tp'))
- input_grad: float32 [4096, 1536], P(('ep', 'tp'))
- norm_gain_grad: float32 [1536], replicated
- query_grad: float32 [1536, 1536], P(None, 'tp')
- key_grad: float32 [1536, 512], P(None, 'tp')
- value_grad: float32 [1536, 512], P(None, 'tp')
- out_grad: float32 [1536, 1536], P('tp')
- moe_gain_grad: float32 [1536], replicated
- router_grad: float32 [1536, 40], replicated
- gate_grad: float32 [40, 1536, 512], P('ep', None, 'tp')
- up_grad: float32 [40, 1536, 512], P('ep', None, 'tp')
- down_grad: float32 [40, 512, 1536], P('ep', 'tp')
Inputs may be any that keep to these rules, and one draw needn't show every extreme that they name: `expert_ids`: each row names 8 different experts. Among the 128 rows of one device (aligned blocks of 128 rows) no expert is named by more than 32 rows, a bound that some block reaches. `segments`: document numbers never fall along a sequence; each document has 1 to 256 tokens, one exactly 256. `valid_mask`: in each sequence the ones form a prefix of 384 tokens or more; the first sequence has no padding.
All inputs are finite; a program needn't handle non-finite values.
Results may differ from a plain program's by a relative error of at most 0.015.
Values may be sent and summed in bfloat16 or wider, within the bound.
No kernel may reach another device: no remote copies, remote signals or barrier semaphores. Data moves between devices by JAX's collectives and lax.ppermute only.
A program may use at most 320 MiB of HBM per device.

v0:
```python
import math
import jax
import jax.numpy as jnp
from jax import lax
from jax.sharding import PartitionSpec as P

HEAD_SIZE_DIM = 64
EPS = 1e-06
HIGH_PRECISION = lax.Precision.HIGHEST


def rms_norm(activation, gain_vec):
    factor = lax.rsqrt(jnp.mean(activation * activation, axis=-1, keepdims=True) + EPS)
    return activation * factor * gain_vec


def rotate(vectors, cos_table, sin_table):
    half_size = vectors.shape[-1] // 2
    first_half = vectors[..., :half_size]
    second_half = vectors[..., half_size:]
    return jnp.concatenate(
        [
            first_half * cos_table - second_half * sin_table,
            second_half * cos_table + first_half * sin_table,
        ],
        axis=-1,
    )


def angle_tables(span_length, head_size):
    half_size = head_size // 2
    inverse = jnp.exp(
        -math.log(10000.0) * jnp.arange(half_size, dtype=jnp.float32) * 2.0 / head_size
    )
    angles = jnp.arange(span_length, dtype=jnp.float32)[:, None] * inverse[None, :]
    return (jnp.cos(angles), jnp.sin(angles))


def swiglu(gate_val, up_val):
    return jax.nn.silu(gate_val) * up_val


def softmax_rows(logits):
    return jax.nn.softmax(logits, axis=-1)


def block_mask(segment_row, live_row, offset, height):
    span_length = segment_row.shape[0]
    key_places = jnp.arange(span_length)
    query_places = offset + jnp.arange(height)
    same_doc = segment_row[:, None] == segment_row[None, :]
    causal = key_places[None, :] <= query_places[:, None]
    usable = (live_row[None, :] > 0) | (key_places[None, :] == query_places[:, None])
    return same_doc & causal & usable


def block_scores(query_block, key_val, allowed, factor):
    scores = (
        jnp.einsum("qgrd,kgd->grqk", query_block, key_val, preferred_element_type=jnp.float32)
        * factor
    )
    return jnp.where(allowed[None, None], scores, -1e30)


def group_rows(boxes):
    return lax.all_gather(boxes, "tp", axis=0, tiled=True)


def dispatch_rows(boxes):
    return lax.all_to_all(boxes, "ep", split_axis=1, concat_axis=1, tiled=True)


def return_rows(boxes):
    return lax.all_to_all(boxes, "ep", split_axis=1, concat_axis=1, tiled=True)


def local(
    tokens,
    norm_gain,
    query_matrix,
    key_matrix,
    value_matrix,
    out_weight,
    moe_gain,
    router_weight,
    gate_weight,
    up_weight,
    down_weight,
    cotangent,
    expert_ids,
    segments,
    valid_mask,
):
    quarter = tokens.shape[0]
    width = tokens.shape[1]
    groups = lax.axis_size("tp")
    owners = lax.axis_size("ep")
    my_part = lax.axis_index("tp")
    seq_len = quarter * groups
    head_size = HEAD_SIZE_DIM
    kv_heads = key_matrix.shape[1] // head_size
    q_heads = query_matrix.shape[1] // head_size
    group_factor = q_heads // kv_heads
    local_experts = gate_weight.shape[0]
    experts_all = router_weight.shape[1]
    chosen_count = expert_ids.shape[1]
    slots = max(8, 3 * quarter * chosen_count // (2 * experts_all) // 8 * 8)
    factor = 1.0 / math.sqrt(head_size)
    segment_row = segments[0]
    live_row = valid_mask[0]
    x_float = tokens.astype(jnp.float32)
    normed = rms_norm(x_float, norm_gain).astype(jnp.bfloat16)
    normed_all = lax.all_gather(normed, "tp", axis=0, tiled=True)
    query_unrotated = jnp.dot(normed_all, query_matrix, preferred_element_type=jnp.float32).reshape(
        seq_len, kv_heads, group_factor, head_size
    )
    key_unrotated = jnp.dot(normed_all, key_matrix, preferred_element_type=jnp.float32).reshape(
        seq_len, kv_heads, head_size
    )
    value_vectors = (
        jnp.dot(normed_all, value_matrix, preferred_element_type=jnp.float32)
        .astype(jnp.bfloat16)
        .reshape(seq_len, kv_heads, head_size)
    )
    cos_table, sin_table = angle_tables(seq_len, head_size)
    cos_query = cos_table[:, None, None, :]
    sin_query = sin_table[:, None, None, :]
    cos_key = cos_table[:, None, :]
    sin_key = sin_table[:, None, :]
    query_val = rotate(query_unrotated, cos_query, sin_query).astype(jnp.bfloat16)
    key_val = rotate(key_unrotated, cos_key, sin_key).astype(jnp.bfloat16)
    height = min(512, seq_len)
    offset = 0
    allowed = block_mask(segment_row, live_row, offset, height)
    scores = block_scores(query_val, key_val, allowed, factor)
    peak = jnp.max(scores, axis=-1, keepdims=True)
    expo = jnp.exp(scores - peak)
    denom = jnp.sum(expo, axis=-1, keepdims=True)
    weights = (expo / denom).astype(jnp.bfloat16)
    mixed = jnp.einsum("grqk,kgd->qgrd", weights, value_vectors, preferred_element_type=jnp.float32)
    outputs = mixed.reshape(height, q_heads * head_size)
    log_sums = [peak + jnp.log(denom)]
    attended = outputs.astype(jnp.bfloat16)
    branch = lax.psum_scatter(
        jnp.dot(attended, out_weight, preferred_element_type=jnp.float32),
        "tp",
        scatter_dimension=0,
        tiled=True,
    )
    middle = x_float + branch
    moe_in = rms_norm(middle, moe_gain).astype(jnp.bfloat16)
    logits = jnp.dot(moe_in, router_weight, preferred_element_type=jnp.float32)
    router = softmax_rows(logits)
    my_valid = lax.dynamic_slice_in_dim(live_row, my_part * quarter, quarter, 0)
    valid_float = my_valid.astype(jnp.float32)
    picked = jnp.take_along_axis(router, expert_ids, axis=1) * valid_float[:, None]
    flat_ids = expert_ids.reshape(-1)
    flat_live = jnp.repeat(my_valid, chosen_count)
    onehot = (flat_ids[:, None] == jnp.arange(experts_all)[None, :]).astype(jnp.int32) * flat_live[
        :, None
    ]
    earlier = jnp.cumsum(onehot, axis=0) - onehot
    slot_of = jnp.sum(earlier * onehot, axis=1)
    target = jnp.where(flat_live > 0, flat_ids, experts_all)
    safe_target = jnp.minimum(target, experts_all - 1)

    def pack(row_block):
        boxes = jnp.zeros((experts_all, slots, width), jnp.bfloat16)
        boxes = boxes.at[target, slot_of].set(row_block, mode="drop")
        return boxes.reshape(1, owners, local_experts * slots, width)

    def unpack(boxes):
        flat_boxes = boxes.reshape(experts_all, slots, width)
        taken = flat_boxes[safe_target, slot_of]
        taken = jnp.where(flat_live[:, None] > 0, taken, jnp.zeros_like(taken))
        return taken.reshape(quarter, chosen_count, width)

    sent = pack(jnp.repeat(moe_in, chosen_count, axis=0))
    full_gate, full_up, full_down = (gate_weight, up_weight, down_weight)
    arrived = dispatch_rows(group_rows(sent))
    expert_rows = arrived.reshape(groups, owners, local_experts, slots, width)
    gate_val = jnp.einsum(
        "tsecd,edf->tsecf", expert_rows, gate_weight, preferred_element_type=jnp.float32
    )
    up_val = jnp.einsum(
        "tsecd,edf->tsecf", expert_rows, up_weight, preferred_element_type=jnp.float32
    )
    hidden = swiglu(gate_val, up_val).astype(jnp.bfloat16)
    result = jnp.einsum("tsecf,efd->tsecd", hidden, down_weight, preferred_element_type=jnp.float32)
    finished = lax.psum_scatter(
        result.reshape(1 * lax.axis_size("tp"), owners, local_experts * slots, width).astype(
            jnp.bfloat16
        ),
        "tp",
        scatter_dimension=0,
        tiled=True,
    )
    returned = lax.dynamic_slice_in_dim(return_rows(group_rows(finished)), my_part, 1, 0)
    result_rows = unpack(returned).astype(jnp.float32)
    output = (middle + jnp.sum(picked[:, :, None] * result_rows, axis=1)).astype(jnp.bfloat16)
    grad_out = cotangent.astype(jnp.float32)
    grad_picked = jnp.einsum("tkd,td->tk", result_rows, grad_out, precision=HIGH_PRECISION)
    onehot_float = (expert_ids[:, :, None] == jnp.arange(experts_all)[None, None, :]).astype(
        jnp.float32
    )
    grad_router = jnp.sum(onehot_float * (grad_picked * valid_float[:, None])[:, :, None], axis=1)
    _, soft_back = jax.vjp(softmax_rows, logits)
    grad_logits = soft_back(grad_router)[0]
    grad_result = (
        (picked[:, :, None] * grad_out[:, None, :])
        .astype(jnp.bfloat16)
        .reshape(quarter * chosen_count, width)
    )
    grad_sent = pack(grad_result)
    grad_arrived = dispatch_rows(group_rows(grad_sent))
    grad_rows = grad_arrived.reshape(groups, owners, local_experts, slots, width)
    gate_all = jnp.einsum(
        "tsecd,edf->tsecf", expert_rows, full_gate, preferred_element_type=jnp.float32
    )
    up_all = jnp.einsum(
        "tsecd,edf->tsecf", expert_rows, full_up, preferred_element_type=jnp.float32
    )
    hidden_all, swiglu_back = jax.vjp(swiglu, gate_all, up_all)
    hidden_low = hidden_all.astype(jnp.bfloat16)
    grad_hidden = jnp.einsum(
        "tsecd,efd->tsecf", grad_rows, full_down, preferred_element_type=jnp.float32
    )
    grad_gate_f, grad_up_f = swiglu_back(grad_hidden)
    grad_gate_rows = grad_gate_f.astype(jnp.bfloat16)
    grad_up_rows = grad_up_f.astype(jnp.bfloat16)
    down_grad = jnp.einsum(
        "tsecf,tsecd->efd", hidden_low, grad_rows, preferred_element_type=jnp.float32
    )
    gate_grad = jnp.einsum(
        "tsecd,tsecf->edf", expert_rows, grad_gate_rows, preferred_element_type=jnp.float32
    )
    up_grad = jnp.einsum(
        "tsecd,tsecf->edf", expert_rows, grad_up_rows, preferred_element_type=jnp.float32
    )
    summed = jnp.einsum(
        "tsecf,edf->tsecd", grad_gate_rows, gate_weight, preferred_element_type=jnp.float32
    )
    summed = summed + jnp.einsum(
        "tsecf,edf->tsecd", grad_up_rows, up_weight, preferred_element_type=jnp.float32
    )
    grad_finished = lax.psum_scatter(
        summed.reshape(1 * lax.axis_size("tp"), owners, local_experts * slots, width).astype(
            jnp.bfloat16
        ),
        "tp",
        scatter_dimension=0,
        tiled=True,
    )
    grad_returned = lax.dynamic_slice_in_dim(return_rows(group_rows(grad_finished)), my_part, 1, 0)
    grad_copies = unpack(grad_returned).astype(jnp.float32)
    router_float = router_weight.astype(jnp.float32)
    grad_moe_in = jnp.sum(grad_copies, axis=1) + jnp.dot(
        grad_logits, router_float.T, precision=HIGH_PRECISION
    )
    router_grad = jnp.dot(moe_in.astype(jnp.float32).T, grad_logits, precision=HIGH_PRECISION)
    _, norm_two_back = jax.vjp(rms_norm, middle, moe_gain)
    grad_mid_norm, moe_gain_grad = norm_two_back(grad_moe_in)
    grad_middle = grad_out + grad_mid_norm
    grad_branch = lax.all_gather(grad_middle.astype(jnp.bfloat16), "tp", axis=0, tiled=True)
    out_grad = jnp.einsum("sh,sd->hd", attended, grad_branch, preferred_element_type=jnp.float32)
    grad_attended = jnp.einsum(
        "sd,hd->sh", grad_branch, out_weight, preferred_element_type=jnp.float32
    ).astype(jnp.bfloat16)
    grad_attended = grad_attended.reshape(seq_len, kv_heads, group_factor, head_size)
    query_parts = []
    key_total = jnp.zeros((seq_len, kv_heads, head_size), jnp.float32)
    value_total = jnp.zeros((seq_len, kv_heads, head_size), jnp.float32)
    for block_no, offset in enumerate(range(0, seq_len, height)):
        allowed = block_mask(segment_row, live_row, offset, height)
        scores = block_scores(query_val, key_val, allowed, factor)
        probs = jnp.where(allowed[None, None], jnp.exp(scores - log_sums[block_no]), 0.0)
        grad_probs = jnp.einsum(
            "qgrd,kgd->grqk", grad_attended, value_vectors, preferred_element_type=jnp.float32
        )
        centre = jnp.sum(probs * grad_probs, axis=-1, keepdims=True)
        grad_scores = (probs * (grad_probs - centre)).astype(jnp.bfloat16)
        query_parts.append(
            jnp.einsum("grqk,kgd->qgrd", grad_scores, key_val, preferred_element_type=jnp.float32)
            * factor
        )
        key_total = (
            jnp.einsum("grqk,qgrd->kgd", grad_scores, query_val, preferred_element_type=jnp.float32)
            * factor
        )
        value_total = jnp.einsum(
            "grqk,qgrd->kgd",
            probs.astype(jnp.bfloat16),
            grad_attended,
            preferred_element_type=jnp.float32,
        )
    grad_query_rot = query_parts[0]
    _, query_back = jax.vjp(lambda vectors: rotate(vectors, cos_query, sin_query), query_unrotated)
    _, key_back = jax.vjp(lambda vectors: rotate(vectors, cos_key, sin_key), key_unrotated)
    grad_q_pre = (
        query_back(grad_query_rot)[0].astype(jnp.bfloat16).reshape(seq_len, q_heads * head_size)
    )
    grad_k_pre = key_back(key_total)[0].astype(jnp.bfloat16).reshape(seq_len, kv_heads * head_size)
    grad_value = value_total.astype(jnp.bfloat16).reshape(seq_len, kv_heads * head_size)
    query_grad = jnp.einsum("sd,sh->dh", normed_all, grad_q_pre, preferred_element_type=jnp.float32)
    key_grad = jnp.einsum("sd,sh->dh", normed_all, grad_k_pre, preferred_element_type=jnp.float32)
    value_grad = jnp.einsum("sd,sh->dh", normed_all, grad_value, preferred_element_type=jnp.float32)
    summed = jnp.einsum("sh,dh->sd", grad_q_pre, query_matrix, preferred_element_type=jnp.float32)
    summed = summed + jnp.einsum(
        "sh,dh->sd", grad_k_pre, key_matrix, preferred_element_type=jnp.float32
    )
    summed = summed + jnp.einsum(
        "sh,dh->sd", grad_value, value_matrix, preferred_element_type=jnp.float32
    )
    grad_normed = lax.psum_scatter(
        summed.astype(jnp.bfloat16), "tp", scatter_dimension=0, tiled=True
    ).astype(jnp.float32)
    _, norm_one_back = jax.vjp(rms_norm, x_float, norm_gain)
    grad_x_norm, norm_gain_grad = norm_one_back(grad_normed)
    input_grad = grad_middle + grad_x_norm
    query_grad, key_grad, value_grad, out_grad = lax.psum(
        (query_grad, key_grad, value_grad, out_grad), "ep"
    )
    norm_gain_grad, moe_gain_grad, router_grad = lax.psum(
        (norm_gain_grad, moe_gain_grad, router_grad), ("ep", "tp")
    )
    return (
        output,
        input_grad,
        norm_gain_grad,
        query_grad,
        key_grad,
        value_grad,
        out_grad,
        moe_gain_grad,
        router_grad,
        gate_grad,
        up_grad,
        down_grad,
    )


def solution(mesh):
    in_specs = (
        P(("ep", "tp"), None),
        P(),
        P(None, "tp"),
        P(None, "tp"),
        P(None, "tp"),
        P("tp", None),
        P(),
        P(),
        P("ep", None, "tp"),
        P("ep", None, "tp"),
        P("ep", "tp", None),
        P(("ep", "tp"), None),
        P(("ep", "tp"), None),
        P("ep", None),
        P("ep", None),
    )
    out_specs = (
        P(("ep", "tp"), None),
        P(("ep", "tp"), None),
        P(),
        P(None, "tp"),
        P(None, "tp"),
        P(None, "tp"),
        P("tp", None),
        P(),
        P(),
        P("ep", None, "tp"),
        P("ep", None, "tp"),
        P("ep", "tp", None),
    )
    return jax.shard_map(local, mesh=mesh, in_specs=in_specs, out_specs=out_specs, check_vma=False)
```

profile of v0, /device:TPU:0, one launch (start us, length us, event | category | flops | bytes accessed | tf_op | source)
XLA Modules:
  0.0 2431.7 jit_solution(11049751359227529653)
XLA Ops:
  7.3 1.3 fusion.70
  9.6 1.9 fusion.66
  13.7 20.4 all-gather.7.cloned.1.call-done
  34.1 2.1 fusion.97
  36.3 2.3 fusion.98
  40.9 1.7 copy-done.4
  45.7 2.7 fusion.99
  51.3 11.3 reduce-window.6
  64.9 21.6 reduce-scatter.5.cloned.1.call-done
  86.6 1.3 multiply_reduce_fusion.3
  89.0 7.0 gather_fusion.2
  96.3 8.4 scatter_custom_fusion.1
  104.7 100.1 %all-gather.13.cloned.1.call-done = bf16[4,8,160,1536]{3,2,1,0:T(8,128)(2,1)} async-done(((bf16[1,8,160,1536]{3,2,1,0:T(8,128)(2,1)}), bf16[4,8,160,1536]{3,2,1,0:T(8,128)(2,1)}) %all-gather.13.cloned.1.call-update) | async-done | bytes 15728656 | tf_op jit(solution)/shard_map/all_gather | solution.py:66
  204.9 13.1 copy.115
  218.0 5.6 all-to-all-start.2
  223.7 8.0 scatter_custom_fusion
  231.7 100.5 %all-gather.9.cloned.1.call-done = bf16[4,8,160,1536]{3,2,1,0:T(8,128)(2,1)} async-done(((bf16[1,8,160,1536]{3,2,1,0:T(8,128)(2,1)}), bf16[4,8,160,1536]{3,2,1,0:T(8,128)(2,1)}) %all-gather.9.cloned.1.call-update) | async-done | bytes 15728656 | tf_op jit(solution)/shard_map/all_gather | solution.py:66
  332.1 13.2 copy.109
  345.4 219.3 %all-to-all-done.2 = bf16[4,8,160,1536]{3,2,0,1:T(8,128)(2,1)} async-done(((bf16[4,8,160,1536]{3,2,0,1:T(8,128)(2,1)}), bf16[4,8,160,1536]{3,2,0,1:T(8,128)(2,1)}, u32[]{:S(2)}, u32[]{:S(2)}) %all-to-all-start.2) | async-done | bytes 15728672 | tf_op jit(solution)/shard_map/all_to_all | solution.py:70
  564.7 6.0 all-to-all-start
  570.8 11.7 fusion.2
  582.5 328.5 %all-to-all-done = bf16[4,8,160,1536]{3,2,0,1:T(8,128)(2,1)} async-done(((bf16[4,8,160,1536]{3,2,0,1:T(8,128)(2,1)}), bf16[4,8,160,1536]{3,2,0,1:T(8,128)(2,1)}, u32[]{:S(2)}, u32[]{:S(2)}) %all-to-all-start) | async-done | bytes 15728672 | tf_op jit(solution)/shard_map/all_to_all | solution.py:70
  911.0 11.7 fusion.6
  922.7 10.5 fusion.33
  933.2 9.8 convert_bitcast_fusion
  942.9 13.3 copy.113
  956.3 118.0 %reduce-scatter.7.cloned.1.call-done = bf16[1,8,160,1536]{3,2,1,0:T(8,128)(2,1)} async-done(((bf16[4,8,160,1536]{3,2,1,0:T(8,128)(2,1)}), bf16[1,8,160,1536]{3,2,1,0:T(8,128)(2,1)}) %reduce-scatter.7.cloned.1.call-update) | async-done | bytes 3932176 | tf_op jit(solution)/shard_map/reduce_scatter | solution.py:190
  1074.5 18.8 fusion.39
  1093.3 18.2 fusion.8
  1111.5 13.4 copy.118
  1125.0 50.9 %all-gather.11.cloned.1.call-done = bf16[4,8,160,1536]{3,2,1,0:T(8,128)(2,1)} async-done(((bf16[1,8,160,1536]{3,2,1,0:T(8,128)(2,1)}), bf16[4,8,160,1536]{3,2,1,0:T(8,128)(2,1)}) %all-gather.11.cloned.1.call-update) | async-done | bytes 15728656 | tf_op jit(solution)/shard_map/all_gather | solution.py:66
  1175.9 13.8 copy.114
  1189.7 6.2 all-to-all-start.1
  1195.9 102.7 %reduce-scatter.9.cloned.1.call-done = bf16[1,8,160,1536]{3,2,1,0:T(8,128)(2,1)} async-done(((bf16[4,8,160,1536]{3,2,1,0:T(8,128)(2,1)}), bf16[1,8,160,1536]{3,2,1,0:T(8,128)(2,1)}) %reduce-scatter.9.cloned.1.call-update) | async-done | bytes 3932176 | tf_op jit(solution)/shard_map/reduce_scatter | solution.py:246
  1298.6 101.6 %all-gather.15.cloned.1.call-done = bf16[4,8,160,1536]{3,2,1,0:T(8,128)(2,1)} async-done(((bf16[1,8,160,1536]{3,2,1,0:T(8,128)(2,1)}), bf16[4,8,160,1536]{3,2,1,0:T(8,128)(2,1)}) %all-gather.15.cloned.1.call-update) | async-done | bytes 15728656 | tf_op jit(solution)/shard_map/all_gather | solution.py:66
  1400.2 13.2 copy.119
  1413.3 123.5 %all-to-all-done.1 = bf16[4,8,160,1536]{3,2,0,1:T(8,128)(2,1)} async-done(((bf16[4,8,160,1536]{3,2,0,1:T(8,128)(2,1)}), bf16[4,8,160,1536]{3,2,0,1:T(8,128)(2,1)}, u32[]{:S(2)}, u32[]{:S(2)}) %all-to-all-start.1) | async-done | bytes 15728672 | tf_op jit(solution)/shard_map/all_to_all | solution.py:74
  1536.9 5.6 all-to-all-start.3
  1542.8 340.0 %all-to-all-done.3 = bf16[4,8,160,1536]{3,2,0,1:T(8,128)(2,1)} async-done(((bf16[4,8,160,1536]{3,2,0,1:T(8,128)(2,1)}), bf16[4,8,160,1536]{3,2,0,1:T(8,128)(2,1)}, u32[]{:S(2)}, u32[]{:S(2)}) %all-to-all-start.3) | async-done | bytes 15728672 | tf_op jit(solution)/shard_map/all_to_all | solution.py:74
  1882.8 7.2 constant_dynamic-slice_fusion
  1890.0 23.2 gather_fusion.1
  1913.2 23.2 gather_fusion
  1936.5 8.4 convert_reduce_fusion
  1945.0 2.4 fusion.46
  1949.9 71.8 %all-gather.17.cloned.1.call-done = bf16[512,1536]{1,0:T(8,128)(2,1)} async-done(((bf16[128,1536]{1,0:T(8,128)(2,1)}), bf16[512,1536]{1,0:T(8,128)(2,1)}) %all-gather.17.cloned.1.call-update) | async-done | bytes 1572880 | tf_op jit(solution)/shard_map/all_gather | solution.py:264
  2021.7 2.7 convolution_convert_fusion
  2024.5 4.8 fusion.58
  2029.2 2.0 fusion.9
  2031.3 1.9 fusion.11
  2037.7 1.8 fusion.28
  2040.9 3.6 fusion.104
  2044.5 1.5 fusion.103
  2046.0 2.4 fusion.101
  2048.4 1.5 fusion.102
  2051.3 10.1 fusion.15
  2061.3 10.8 convolution_bitcast_fusion.1
  2072.3 10.8 convolution_bitcast_fusion
  2083.1 1.4 fusion.67
  2084.5 39.3 %all-reduce.4 = (f32[1536]{0:T(1024)}, f32[1536]{0:T(1024)}) all-reduce(f32[1536]{0:T(1024)S(1)} %get-tuple-element.14, f32[1536]{0:T(1024)S(1)} %get-tuple-element.12), channel_id=1, replica_groups=mesh['ep'=8,'tp'=4] {'ep','tp'}, use_global_device_ids=true, to_apply=%region_23.24 | all-reduce | flops 3072 | bytes 24576 | tf_op jit(solution)/shard_map/psum | solution.py:323
  2123.8 2.4 fusion.69
  2126.2 71.5 %all-reduce.9.cloned.1.call-done = f32[1536,40]{0,1:T(8,128)} async-done(((f32[1536,40]{0,1:T(8,128)}), f32[1536,40]{0,1:T(8,128)}) %all-reduce.9.cloned.1.call-update) | async-done | bytes 245776 | tf_op jit(solution)/shard_map/psum | solution.py:323
  2197.7 219.5 %all-reduce.11.cloned.1.call-done = (f32[1536,384]{1,0:T(8,128)}, f32[1536,128]{1,0:T(8,128)}, f32[1536,128]{1,0:T(8,128)}, f32[384,1536]{1,0:T(8,128)}) async-done(((f32[1536,384]{1,0:T(8,128)}, f32[1536,128]{1,0:T(8,128)}, f32[1536,128]{1,0:T(8,128)}, f32[384,1536]{1,0:T(8,128)}), (f32[1536,384]{1,0:T(8,128)}, f32[1536,128]{1,0:T(8,128)}, f32[1536,128]{1,0:T(8,128)}, ...) | async-done | bytes 6291472 | tf_op jit(solution)/shard_map/psum | solution.py:320
  2417.2 3.4 copy.188
  2422.4 1.4 copy.191
  (280 shorter events, 27.4 us)
Async XLA Ops:
  7.2 915.5 %copy-start = (bf16[5,1536,128]{2,1,0:T(8,128)(2,1)S(1)}, bf16[5,1536,128]{2,1,0:T(8,128)(2,1)}, u32[]{:S(2)}) copy-start(bf16[5,1536,128]{2,1,0:T(8,128)(2,1)} %param.24) | copy-start | bytes 5898244
  7.2 29.1 %copy-start.40 = (bf16[1536,384]{1,0:T(8,128)(2,1)S(1)}, bf16[1536,384]{1,0:T(8,128)(2,1)}, u32[]{:S(2)}) copy-start(bf16[1536,384]{1,0:T(8,128)(2,1)} %param.17) | copy-start | bytes 3538948
  7.2 26.9 %all-gather.7.cloned.1.call-start = ((), (), s32[]{:S(2)}) async-start(), calls=%async_computation.8 | async-start | bytes 1966080 | tf_op jit(solution)/shard_map/all_gather | solution.py:113
  11.6 75.0 %reduce-scatter.5.cloned.1.call-start = ((), (), s32[]{:S(2)}) async-start(), calls=%async_computation.9 | async-start | bytes 3932160 | tf_op jit(solution)/shard_map/reduce_scatter | solution.py:144
  12.7 25.9 %copy-start.28 = (f32[512,32]{0,1:T(8,128)}, f32[512,32]{0,1:T(8,128)S(1)}, u32[]{:S(2)}) copy-start(f32[512,32]{0,1:T(8,128)S(1)} %get-tuple-element.45) | copy-start | bytes 196612
  12.7 25.9 %copy-start.30 = (f32[512,32]{0,1:T(8,128)}, f32[512,32]{0,1:T(8,128)S(1)}, u32[]{:S(2)}) copy-start(f32[512,32]{0,1:T(8,128)S(1)} %get-tuple-element.46) | copy-start | bytes 196612
  13.7 25.1 %copy-start.16 = (pred[512,512]{0,1:T(8,128)(4,1)}, pred[512,512]{0,1:T(8,128)(4,1)S(1)}, u32[]{:S(2)}) copy-start(pred[512,512]{0,1:T(8,128)(4,1)S(1)} %fusion.62) | copy-start | bytes 786436
  36.3 3.7 copy-start.57
  36.3 3.7 copy-start.59
  40.0 3.7 copy-start.3
  40.0 3.7 copy-start.65
  48.3 14.6 copy-start.18
  48.3 16.4 copy-start.88
  48.3 16.5 copy-start.87
  48.3 38.2 %copy-start.10 = (bf16[128,1536]{1,0:T(8,128)(2,1)S(1)}, bf16[128,1536]{1,0:T(8,128)(2,1)}, u32[]{:S(2)}) copy-start(bf16[128,1536]{1,0:T(8,128)(2,1)} %param.15) | copy-start | bytes 1179652
  48.4 39.5 %copy-start.62 = (f32[1536]{0:T(1024)S(1)}, f32[1536]{0:T(1024)}, u32[]{:S(2)}) copy-start(f32[1536]{0:T(1024)} %param.21) | copy-start | bytes 18436
  48.4 156.5 %all-gather.13.cloned.1.call-start = ((), (), s32[]{:S(2)}) async-start(), calls=%async_computation.13 | async-start | bytes 19660800 | tf_op jit(solution)/shard_map/all_gather | solution.py:66
  50.0 46.1 %copy-start.77 = (f32[128]{0:T(128)}, f32[128]{0:T(128)S(1)}, u32[]{:S(2)}) copy-start(f32[128]{0:T(128)S(1)} %get-tuple-element.24) | copy-start | bytes 1540
  50.8 37.3 %copy-start.55 = (bf16[1536,40]{0,1:T(8,128)(2,1)S(1)}, bf16[1536,40]{0,1:T(8,128)(2,1)}, u32[]{:S(2)}) copy-start(bf16[1536,40]{0,1:T(8,128)(2,1)} %param.22) | copy-start | bytes 368644
  88.1 135.6 %copy-start.14 = (bf16[128,1536]{1,0:T(8,128)(2,1)}, bf16[128,1536]{1,0:T(8,128)(2,1)S(1)}, u32[]{:S(2)}) copy-start(bf16[128,1536]{1,0:T(8,128)(2,1)S(1)} %multiply_convert_fusion) | copy-start | bytes 1179652
  89.0 7.1 copy-start.75
  89.0 7.3 copy-start.23
  96.2 8.5 copy-start.50
  218.0 346.7 %all-to-all-start.2 = ((bf16[4,8,160,1536]{3,2,0,1:T(8,128)(2,1)}), bf16[4,8,160,1536]{3,2,0,1:T(8,128)(2,1)}, u32[]{:S(2)}, u32[]{:S(2)}) async-start(bf16[4,8,160,1536]{3,2,0,1:T(8,128)(2,1)} %copy.115), calls=%async_computation.4 | async-start | bytes 31457280 | tf_op jit(solution)/shard_map/all_to_all | solution.py:70
  223.6 108.5 %all-gather.9.cloned.1.call-start = ((), (), s32[]{:S(2)}) async-start(), calls=%async_computation.10 | async-start | bytes 19660800 | tf_op jit(solution)/shard_map/all_gather | solution.py:66
  564.7 346.3 %all-to-all-start = ((bf16[4,8,160,1536]{3,2,0,1:T(8,128)(2,1)}), bf16[4,8,160,1536]{3,2,0,1:T(8,128)(2,1)}, u32[]{:S(2)}, u32[]{:S(2)}) async-start(bf16[4,8,160,1536]{3,2,0,1:T(8,128)(2,1)} %copy.109), calls=%async_computation.1 | async-start | bytes 31457280 | tf_op jit(solution)/shard_map/all_to_all | solution.py:70
  570.7 503.6 %reduce-scatter.7.cloned.1.call-start = ((), (), s32[]{:S(2)}) async-start(), calls=%async_computation.11 | async-start | bytes 19660800 | tf_op jit(solution)/shard_map/reduce_scatter | solution.py:190
  933.2 9.8 copy-start.26
  956.3 118.2 %copy-start.37 = (bf16[4,8,5,32,128]{4,3,1,0,2:T(8,128)(2,1)S(1)}, bf16[4,8,5,32,128]{4,3,1,0,2:T(8,128)(2,1)}, u32[]{:S(2)}) copy-start(bf16[4,8,5,32,128]{4,3,1,0,2:T(8,128)(2,1)} %get-tuple-element.29) | copy-start | bytes 3932164
  956.3 219.6 %all-gather.11.cloned.1.call-start = ((), (), s32[]{:S(2)}) async-start(), calls=%async_computation.12 | async-start | bytes 19660800 | tf_op jit(solution)/shard_map/all_gather | solution.py:66
  1074.4 224.1 %reduce-scatter.9.cloned.1.call-start = ((), (), s32[]{:S(2)}) async-start(), calls=%async_computation.14 | async-start | bytes 19660800 | tf_op jit(solution)/shard_map/reduce_scatter | solution.py:246
  1074.5 18.8 copy-start.35
  1189.7 347.2 %all-to-all-start.1 = ((bf16[4,8,160,1536]{3,2,0,1:T(8,128)(2,1)}), bf16[4,8,160,1536]{3,2,0,1:T(8,128)(2,1)}, u32[]{:S(2)}, u32[]{:S(2)}) async-start(bf16[4,8,160,1536]{3,2,0,1:T(8,128)(2,1)} %copy.114), calls=%async_computation.3 | async-start | bytes 31457280 | tf_op jit(solution)/shard_map/all_to_all | solution.py:74
  1195.8 204.4 %all-gather.15.cloned.1.call-start = ((), (), s32[]{:S(2)}) async-start(), calls=%async_computation.15 | async-start | bytes 19660800 | tf_op jit(solution)/shard_map/all_gather | solution.py:66
  1413.3 129.4 %copy-start.76 = (f32[128]{0:T(128)S(1)}, f32[128]{0:T(128)}, u32[]{:S(2)}) copy-start(f32[128]{0:T(128)} %copy-done.75) | copy-start | bytes 1540
  1536.9 345.9 %all-to-all-start.3 = ((bf16[4,8,160,1536]{3,2,0,1:T(8,128)(2,1)}), bf16[4,8,160,1536]{3,2,0,1:T(8,128)(2,1)}, u32[]{:S(2)}, u32[]{:S(2)}) async-start(bf16[4,8,160,1536]{3,2,0,1:T(8,128)(2,1)} %copy.119), calls=%async_computation.6 | async-start | bytes 31457280 | tf_op jit(solution)/shard_map/all_to_all | solution.py:74
  1542.5 479.2 %all-gather.17.cloned.1.call-start = ((), (), s32[]{:S(2)}) async-start(), calls=%async_computation.16 | async-start | bytes 1966080 | tf_op jit(solution)/shard_map/all_gather | solution.py:264
  1542.8 347.2 %copy-start.2 = (s32[1024,1]{0,1:T(1,128)S(1)}, s32[1024,1]{0,1:T(1,128)}, u32[]{:S(2)}) copy-start(s32[1024,1]{0,1:T(1,128)} %get-tuple-element.41) | copy-start | bytes 12292
  1913.2 23.2 copy-start.51
  1913.2 23.2 copy-start.82
  1936.5 8.4 copy-start.9
  1936.5 8.4 copy-start.19
  1948.5 75.9 %copy-start.12 = (f32[128,1536]{1,0:T(8,128)}, f32[128,1536]{1,0:T(8,128)S(1)}, u32[]{:S(2)}) copy-start(f32[128,1536]{1,0:T(8,128)S(1)} %get-tuple-element.51) | copy-start | bytes 2359300
  1949.6 74.9 %copy-start.17 = (pred[512,512]{0,1:T(8,128)(4,1)S(1)}, pred[512,512]{0,1:T(8,128)(4,1)}, u32[]{:S(2)}) copy-start(pred[512,512]{0,1:T(8,128)(4,1)} %copy-done.16) | copy-start | bytes 786436
  1949.6 133.5 %reduce-scatter.11.cloned.1.call-start = ((), (), s32[]{:S(2)}) async-start(), calls=%async_computation.17 | async-start | bytes 1966080 | tf_op jit(solution)/shard_map/reduce_scatter | solution.py:314
  2021.7 7.5 slice-start
  2024.4 4.8 slice-start.1
  2024.4 4.8 copy-start.54
  2039.5 5.0 copy-start.5
  2039.5 158.2 %all-reduce.9.cloned.1.call-start = ((), (), s32[]{:S(2)}) async-start(), calls=%async_computation.18 | async-start | bytes 491520 | tf_op jit(solution)/shard_map/psum | solution.py:323
  2040.6 376.6 %all-reduce.11.cloned.1.call-start = ((), (), s32[]{:S(2)}) async-start(), calls=%async_computation.19 | async-start | bytes 12582912 | tf_op jit(solution)/shard_map/psum | solution.py:320
  2051.3 10.1 copy-start.38
  2061.3 10.8 copy-start.36
  2072.2 10.9 copy-start.11
  2072.2 10.9 copy-start.64
  2072.2 10.9 copy-start.80
  2072.2 51.6 %copy-start.84 = (f32[128]{0:T(128)S(1)}, f32[128]{0:T(128)}, u32[]{:S(2)}) copy-start(f32[128]{0:T(128)} %copy-done.83) | copy-start | bytes 1540
  2072.2 51.6 %copy-start.8 = (f32[128,1536]{1,0:T(8,128)S(1)}, f32[128,1536]{1,0:T(8,128)}, u32[]{:S(2)}) copy-start(f32[128,1536]{1,0:T(8,128)} %copy-done.6) | copy-start | bytes 2359300
  2072.2 51.6 %copy-start.13 = (f32[128,1536]{1,0:T(8,128)S(1)}, f32[128,1536]{1,0:T(8,128)}, u32[]{:S(2)}) copy-start(f32[128,1536]{1,0:T(8,128)} %copy-done.12) | copy-start | bytes 2359300
  2072.2 51.6 %copy-start.20 = (bf16[128,1536]{1,0:T(8,128)(2,1)S(1)}, bf16[128,1536]{1,0:T(8,128)(2,1)}, u32[]{:S(2)}) copy-start(bf16[128,1536]{1,0:T(8,128)(2,1)} %param.26) | copy-start | bytes 1179652
  2072.2 51.6 %copy-start.24 = (f32[128,1536]{1,0:T(8,128)S(1)}, f32[128,1536]{1,0:T(8,128)}, u32[]{:S(2)}) copy-start(f32[128,1536]{1,0:T(8,128)} %get-tuple-element.17) | copy-start | bytes 2359300
  2417.2 4.3 copy-start.42
  2417.2 5.1 copy-start.25
  2420.6 3.9 copy-start.1
  (43 other events, 76.7 us)
Sparse Core Ops, SparseCore 0:
  11.7 22.3 all-gather.6
  48.5 38.0 reduce-scatter.4
  104.8 99.9 all-gather.12
  231.8 100.3 all-gather.8
  956.4 117.9 reduce-scatter.6
  1075.9 99.9 all-gather.10
  1178.6 119.8 reduce-scatter.8
  1300.2 99.9 all-gather.14
  1949.7 71.9 all-gather.16
  2039.6 28.1 reduce-scatter.10
  2073.9 123.6 all-reduce.8
  2202.5 214.6 all-reduce.10
where the time goes:
time: 2440 us; the launch traced here: 2430 us
  waiting for transfers between devices  1990 us (82%)
  local copies, waits for them, and re-layouts  165 us (7%)
  matrix products  151 us (6%)
  other arithmetic  45.8 us (2%)
  blocking collectives  39.3 us (2%)
  starting transfers between devices  24.8 us (1%)
    all_to_all x2, waiting for transfers between devices, dispatch_rows(): return lax.all_to_all(boxes, 'ep', split_axis=1, concat_axis=1, tiled=True)  548 us
    all_to_all x2, waiting for transfers between devices, return_rows(): return lax.all_to_all(boxes, 'ep', split_axis=1, concat_axis=1, tiled=True)  464 us
    all_gather x4, waiting for transfers between devices, group_rows(): return lax.all_gather(boxes, 'tp', axis=0, tiled=True)  353 us
    psum x1, waiting for transfers between devices, local(): lax.psum((query_grad, key_grad, value_grad, out_grad), 'ep')  220 us
    reduce_scatter x1, waiting for transfers between devices, local(): lax.psum_scatter(result.reshape(1 * lax.axis_size('tp'), owners, local_ex...  118 us
    reduce_scatter x1, waiting for transfers between devices, local(): lax.psum_scatter(summed.reshape(1 * lax.axis_size('tp'), owners, local_ex...  103 us
    all_gather x1, waiting for transfers between devices, local(): lax.all_gather(grad_middle.astype(jnp.bfloat16), 'tp', axis=0, tiled=True)  71.8 us
    psum x1, waiting for transfers between devices, local(): lax.psum((norm_gain_grad, moe_gain_grad, router_grad), ('ep', 'tp'))  71.5 us
  transfers between devices with their start and end apart: 16, of which 15 were waited for; matrix products, arithmetic and copies ran while one was open for 7% of the time, Pallas kernels for 0%

commit v1 on v0

--- a/solution.py
+++ b/solution.py
@@ -321,7 +321,7 @@
         (query_grad, key_grad, value_grad, out_grad), "ep"
     )
     norm_gain_grad, moe_gain_grad, router_grad = lax.psum(
-        (norm_gain_grad, moe_gain_grad, router_grad), ("ep", "tp")
+        lax.psum((norm_gain_grad, moe_gain_grad, router_grad), "tp"), "ep"
     )
     return (
         output,

time: 2440 us -> 2340 us (0.959)
  waiting for transfers between devices: 1990 us -> 1880 us
    psum x1, waiting for transfers between devices: 71.5 us -> 9.26 us  [local(): lax.psum((norm_gain_grad, moe_gain_grad, router_grad), 'tp')]
    psum x1, waiting for transfers between devices: 220 us -> 174 us  [local(): lax.psum((query_grad, key_grad, value_grad, out_grad), 'ep')]
    psum x1 -> x2, blocking collectives: 39.3 us -> 50.4 us  [the longest x1 40.2 us: local(): lax.psum(lax.psum((norm_gain_grad, moe_gain_grad, router_grad), 'tp'), 'ep')]
  transfers between devices with their start and end apart: 16 -> 16, of which waited for: 15 -> 15; matrix products, arithmetic and copies ran while one was open for 7% -> 8% of each run, Pallas kernels for 0% -> 0%
where the time goes in v1:
time: 2340 us; the launch traced here: 2330 us
  waiting for transfers between devices  1880 us (80%)
  local copies, waits for them, and re-layouts  166 us (7%)
  matrix products  149 us (6%)
  blocking collectives  50.4 us (2%)
  other arithmetic  47.3 us (2%)
  starting transfers between devices  24.8 us (1%)
    all_to_all x2, waiting for transfers between devices, dispatch_rows(): return lax.all_to_all(boxes, 'ep', split_axis=1, concat_axis=1, tiled=True)  548 us
    all_to_all x2, waiting for transfers between devices, return_rows(): return lax.all_to_all(boxes, 'ep', split_axis=1, concat_axis=1, tiled=True)  464 us
    all_gather x4, waiting for transfers between devices, group_rows(): return lax.all_gather(boxes, 'tp', axis=0, tiled=True)  353 us
    psum x1, waiting for transfers between devices, local(): lax.psum((query_grad, key_grad, value_grad, out_grad), 'ep')  174 us
    reduce_scatter x1, waiting for transfers between devices, local(): lax.psum_scatter(result.reshape(1 * lax.axis_size('tp'), owners, local_ex...  118 us
    reduce_scatter x1, waiting for transfers between devices, local(): lax.psum_scatter(summed.reshape(1 * lax.axis_size('tp'), owners, local_ex...  103 us
    all_gather x1, waiting for transfers between devices, local(): lax.all_gather(grad_middle.astype(jnp.bfloat16), 'tp', axis=0, tiled=True)  69.3 us
    all_gather x4, local copies, waits for them, and re-layouts, group_rows(): return lax.all_gather(boxes, 'tp', axis=0, tiled=True)  53.3 us
  transfers between devices with their start and end apart: 16, of which 15 were waited for; matrix products, arithmetic and copies ran while one was open for 8% of the time, Pallas kernels for 0%

profile of v1, /device:TPU:0, one launch (start us, length us, event | category | flops | bytes accessed | tf_op | source)
XLA Modules:
  0.0 2333.2 jit_solution(10337978898196453238)
XLA Ops:
  9.7 1.9 fusion.66
  13.7 20.4 all-gather.7.cloned.1.call-done
  34.1 2.1 fusion.97
  36.3 2.3 fusion.98
  41.0 1.7 copy-done.4
  45.7 2.7 fusion.99
  51.4 11.3 reduce-window.6
  65.0 21.6 reduce-scatter.5.cloned.1.call-done
  89.0 7.0 gather_fusion.2
  96.3 8.4 scatter_custom_fusion.1
  104.7 100.1 %all-gather.13.cloned.1.call-done = bf16[4,8,160,1536]{3,2,1,0:T(8,128)(2,1)} async-done(((bf16[1,8,160,1536]{3,2,1,0:T(8,128)(2,1)}), bf16[4,8,160,1536]{3,2,1,0:T(8,128)(2,1)}) %all-gather.13.cloned.1.call-update) | async-done | bytes 15728656 | tf_op jit(solution)/shard_map/all_gather | solution.py:66
  204.8 13.1 copy.115
  217.9 5.6 all-to-all-start.2
  223.6 8.0 scatter_custom_fusion
  231.6 100.5 %all-gather.9.cloned.1.call-done = bf16[4,8,160,1536]{3,2,1,0:T(8,128)(2,1)} async-done(((bf16[1,8,160,1536]{3,2,1,0:T(8,128)(2,1)}), bf16[4,8,160,1536]{3,2,1,0:T(8,128)(2,1)}) %all-gather.9.cloned.1.call-update) | async-done | bytes 15728656 | tf_op jit(solution)/shard_map/all_gather | solution.py:66
  332.1 13.2 copy.109
  345.3 219.3 %all-to-all-done.2 = bf16[4,8,160,1536]{3,2,0,1:T(8,128)(2,1)} async-done(((bf16[4,8,160,1536]{3,2,0,1:T(8,128)(2,1)}), bf16[4,8,160,1536]{3,2,0,1:T(8,128)(2,1)}, u32[]{:S(2)}, u32[]{:S(2)}) %all-to-all-start.2) | async-done | bytes 15728672 | tf_op jit(solution)/shard_map/all_to_all | solution.py:70
  564.6 6.0 all-to-all-start
  570.7 11.7 fusion.2
  582.4 328.5 %all-to-all-done = bf16[4,8,160,1536]{3,2,0,1:T(8,128)(2,1)} async-done(((bf16[4,8,160,1536]{3,2,0,1:T(8,128)(2,1)}), bf16[4,8,160,1536]{3,2,0,1:T(8,128)(2,1)}, u32[]{:S(2)}, u32[]{:S(2)}) %all-to-all-start) | async-done | bytes 15728672 | tf_op jit(solution)/shard_map/all_to_all | solution.py:70
  910.9 11.7 fusion.6
  922.6 10.5 fusion.33
  933.1 9.7 convert_bitcast_fusion
  942.8 13.3 copy.113
  956.2 118.0 %reduce-scatter.7.cloned.1.call-done = bf16[1,8,160,1536]{3,2,1,0:T(8,128)(2,1)} async-done(((bf16[4,8,160,1536]{3,2,1,0:T(8,128)(2,1)}), bf16[1,8,160,1536]{3,2,1,0:T(8,128)(2,1)}) %reduce-scatter.7.cloned.1.call-update) | async-done | bytes 3932176 | tf_op jit(solution)/shard_map/reduce_scatter | solution.py:190
  1074.3 18.8 fusion.39
  1093.1 18.3 fusion.8
  1111.4 13.4 copy.118
  1124.9 50.9 %all-gather.11.cloned.1.call-done = bf16[4,8,160,1536]{3,2,1,0:T(8,128)(2,1)} async-done(((bf16[1,8,160,1536]{3,2,1,0:T(8,128)(2,1)}), bf16[4,8,160,1536]{3,2,1,0:T(8,128)(2,1)}) %all-gather.11.cloned.1.call-update) | async-done | bytes 15728656 | tf_op jit(solution)/shard_map/all_gather | solution.py:66
  1175.7 13.8 copy.114
  1189.5 6.2 all-to-all-start.1
  1195.7 102.6 %reduce-scatter.9.cloned.1.call-done = bf16[1,8,160,1536]{3,2,1,0:T(8,128)(2,1)} async-done(((bf16[4,8,160,1536]{3,2,1,0:T(8,128)(2,1)}), bf16[1,8,160,1536]{3,2,1,0:T(8,128)(2,1)}) %reduce-scatter.9.cloned.1.call-update) | async-done | bytes 3932176 | tf_op jit(solution)/shard_map/reduce_scatter | solution.py:246
  1298.4 101.6 %all-gather.15.cloned.1.call-done = bf16[4,8,160,1536]{3,2,1,0:T(8,128)(2,1)} async-done(((bf16[1,8,160,1536]{3,2,1,0:T(8,128)(2,1)}), bf16[4,8,160,1536]{3,2,1,0:T(8,128)(2,1)}) %all-gather.15.cloned.1.call-update) | async-done | bytes 15728656 | tf_op jit(solution)/shard_map/all_gather | solution.py:66
  1400.0 13.2 copy.119
  1413.2 123.6 %all-to-all-done.1 = bf16[4,8,160,1536]{3,2,0,1:T(8,128)(2,1)} async-done(((bf16[4,8,160,1536]{3,2,0,1:T(8,128)(2,1)}), bf16[4,8,160,1536]{3,2,0,1:T(8,128)(2,1)}, u32[]{:S(2)}, u32[]{:S(2)}) %all-to-all-start.1) | async-done | bytes 15728672 | tf_op jit(solution)/shard_map/all_to_all | solution.py:74
  1536.7 5.6 all-to-all-start.3
  1542.6 340.0 %all-to-all-done.3 = bf16[4,8,160,1536]{3,2,0,1:T(8,128)(2,1)} async-done(((bf16[4,8,160,1536]{3,2,0,1:T(8,128)(2,1)}), bf16[4,8,160,1536]{3,2,0,1:T(8,128)(2,1)}, u32[]{:S(2)}, u32[]{:S(2)}) %all-to-all-start.3) | async-done | bytes 15728672 | tf_op jit(solution)/shard_map/all_to_all | solution.py:74
  1882.6 7.2 constant_dynamic-slice_fusion
  1889.9 23.2 gather_fusion.1
  1913.1 23.2 gather_fusion
  1936.3 8.4 convert_reduce_fusion
  1944.8 2.4 fusion.46
  1952.5 1.7 fusion.91
  1954.6 69.3 %all-gather.17.cloned.1.call-done = bf16[512,1536]{1,0:T(8,128)(2,1)} async-done(((bf16[128,1536]{1,0:T(8,128)(2,1)}), bf16[512,1536]{1,0:T(8,128)(2,1)}) %all-gather.17.cloned.1.call-update) | async-done | bytes 1572880 | tf_op jit(solution)/shard_map/all_gather | solution.py:264
  2023.8 2.4 convolution_convert_fusion
  2026.2 4.1 fusion.58
  2030.4 2.0 fusion.9
  2032.4 1.9 fusion.11
  2038.8 1.8 fusion.28
  2040.9 1.5 fusion.103
  2042.4 1.5 fusion.102
  2043.9 2.2 fusion.104
  2046.1 2.4 fusion.101
  2048.5 9.3 all-reduce.10.cloned.1.call-done
  2059.1 9.8 fusion.15
  2068.9 10.9 convolution_bitcast_fusion.1
  2080.0 10.9 convolution_bitcast_fusion
  2090.8 1.4 fusion.67
  2092.2 10.2 all-reduce.6
  2102.4 40.2 %all-reduce.4 = (f32[1536]{0:T(1024)}, f32[1536]{0:T(1024)}) all-reduce(f32[1536]{0:T(1024)S(1)} %get-tuple-element.25, f32[1536]{0:T(1024)S(1)} %get-tuple-element.26), channel_id=1, replica_groups=mesh['ep'=8,'tp'=4] {'ep'}, use_global_device_ids=true, to_apply=%region_24.25 | all-reduce | flops 3072 | bytes 24576 | tf_op jit(solution)/shard_map/psum | solution.py:323
  2142.6 2.4 fusion.69
  2145.0 173.6 %all-reduce.12.cloned.1.call-done = (f32[1536,384]{1,0:T(8,128)}, f32[1536,128]{1,0:T(8,128)}, f32[1536,128]{1,0:T(8,128)}, f32[384,1536]{1,0:T(8,128)}, f32[1536,40]{0,1:T(8,128)}) async-done(((f32[1536,384]{1,0:T(8,128)}, f32[1536,128]{1,0:T(8,128)}, f32[1536,128]{1,0:T(8,128)}, f32[384,1536]{1,0:T(8,128)}, f32[1536,40]{0,1:T(8,128)}), (f32[1536,384]{1,0:T(8,128)}, f32[1536,128]{1,0:T(8,128)}, ...) | async-done | bytes 6537232 | tf_op jit(solution)/shard_map/psum | solution.py:320
  2318.6 3.4 copy.189
  2323.8 1.4 copy.192
  (287 shorter events, 32.2 us)
Async XLA Ops:
  7.2 915.5 %copy-start = (bf16[5,1536,128]{2,1,0:T(8,128)(2,1)S(1)}, bf16[5,1536,128]{2,1,0:T(8,128)(2,1)}, u32[]{:S(2)}) copy-start(bf16[5,1536,128]{2,1,0:T(8,128)(2,1)} %param.24) | copy-start | bytes 5898244
  7.2 29.1 %copy-start.42 = (bf16[1536,384]{1,0:T(8,128)(2,1)S(1)}, bf16[1536,384]{1,0:T(8,128)(2,1)}, u32[]{:S(2)}) copy-start(bf16[1536,384]{1,0:T(8,128)(2,1)} %param.17) | copy-start | bytes 3538948
  7.2 26.9 %all-gather.7.cloned.1.call-start = ((), (), s32[]{:S(2)}) async-start(), calls=%async_computation.8 | async-start | bytes 1966080 | tf_op jit(solution)/shard_map/all_gather | solution.py:113
  11.6 74.9 %reduce-scatter.5.cloned.1.call-start = ((), (), s32[]{:S(2)}) async-start(), calls=%async_computation.9 | async-start | bytes 3932160 | tf_op jit(solution)/shard_map/reduce_scatter | solution.py:144
  12.7 25.9 %copy-start.28 = (f32[512,32]{0,1:T(8,128)}, f32[512,32]{0,1:T(8,128)S(1)}, u32[]{:S(2)}) copy-start(f32[512,32]{0,1:T(8,128)S(1)} %get-tuple-element.48) | copy-start | bytes 196612
  12.7 25.9 %copy-start.30 = (f32[512,32]{0,1:T(8,128)}, f32[512,32]{0,1:T(8,128)S(1)}, u32[]{:S(2)}) copy-start(f32[512,32]{0,1:T(8,128)S(1)} %get-tuple-element.49) | copy-start | bytes 196612
  13.7 25.1 %copy-start.16 = (pred[512,512]{0,1:T(8,128)(4,1)}, pred[512,512]{0,1:T(8,128)(4,1)S(1)}, u32[]{:S(2)}) copy-start(pred[512,512]{0,1:T(8,128)(4,1)S(1)} %fusion.62) | copy-start | bytes 786436
  36.3 3.7 copy-start.59
  48.4 14.6 copy-start.18
  48.4 16.4 copy-start.91
  48.4 16.5 copy-start.90
  48.4 38.2 %copy-start.10 = (bf16[128,1536]{1,0:T(8,128)(2,1)S(1)}, bf16[128,1536]{1,0:T(8,128)(2,1)}, u32[]{:S(2)}) copy-start(bf16[128,1536]{1,0:T(8,128)(2,1)} %param.15) | copy-start | bytes 1179652
  48.4 39.5 %copy-start.64 = (f32[1536]{0:T(1024)S(1)}, f32[1536]{0:T(1024)}, u32[]{:S(2)}) copy-start(f32[1536]{0:T(1024)} %param.21) | copy-start | bytes 18436
  48.4 156.4 %all-gather.13.cloned.1.call-start = ((), (), s32[]{:S(2)}) async-start(), calls=%async_computation.13 | async-start | bytes 19660800 | tf_op jit(solution)/shard_map/all_gather | solution.py:66
  50.0 46.1 %copy-start.78 = (f32[128]{0:T(128)}, f32[128]{0:T(128)S(1)}, u32[]{:S(2)}) copy-start(f32[128]{0:T(128)S(1)} %get-tuple-element.27) | copy-start | bytes 1540
  50.8 37.2 %copy-start.56 = (bf16[1536,40]{0,1:T(8,128)(2,1)S(1)}, bf16[1536,40]{0,1:T(8,128)(2,1)}, u32[]{:S(2)}) copy-start(bf16[1536,40]{0,1:T(8,128)(2,1)} %param.22) | copy-start | bytes 368644
  88.1 135.5 %copy-start.14 = (bf16[128,1536]{1,0:T(8,128)(2,1)}, bf16[128,1536]{1,0:T(8,128)(2,1)S(1)}, u32[]{:S(2)}) copy-start(bf16[128,1536]{1,0:T(8,128)(2,1)S(1)} %multiply_convert_fusion) | copy-start | bytes 1179652
  88.9 7.1 copy-start.76
  88.9 7.3 copy-start.23
  96.2 8.5 copy-start.52
  217.9 346.7 %all-to-all-start.2 = ((bf16[4,8,160,1536]{3,2,0,1:T(8,128)(2,1)}), bf16[4,8,160,1536]{3,2,0,1:T(8,128)(2,1)}, u32[]{:S(2)}, u32[]{:S(2)}) async-start(bf16[4,8,160,1536]{3,2,0,1:T(8,128)(2,1)} %copy.115), calls=%async_computation.4 | async-start | bytes 31457280 | tf_op jit(solution)/shard_map/all_to_all | solution.py:70
  223.6 108.5 %all-gather.9.cloned.1.call-start = ((), (), s32[]{:S(2)}) async-start(), calls=%async_computation.10 | async-start | bytes 19660800 | tf_op jit(solution)/shard_map/all_gather | solution.py:66
  564.6 346.3 %all-to-all-start = ((bf16[4,8,160,1536]{3,2,0,1:T(8,128)(2,1)}), bf16[4,8,160,1536]{3,2,0,1:T(8,128)(2,1)}, u32[]{:S(2)}, u32[]{:S(2)}) async-start(bf16[4,8,160,1536]{3,2,0,1:T(8,128)(2,1)} %copy.109), calls=%async_computation.1 | async-start | bytes 31457280 | tf_op jit(solution)/shard_map/all_to_all | solution.py:70
  570.7 503.5 %reduce-scatter.7.cloned.1.call-start = ((), (), s32[]{:S(2)}) async-start(), calls=%async_computation.11 | async-start | bytes 19660800 | tf_op jit(solution)/shard_map/reduce_scatter | solution.py:190
  933.1 9.7 copy-start.26
  956.1 118.2 %copy-start.38 = (bf16[4,8,5,32,128]{4,3,1,0,2:T(8,128)(2,1)S(1)}, bf16[4,8,5,32,128]{4,3,1,0,2:T(8,128)(2,1)}, u32[]{:S(2)}) copy-start(bf16[4,8,5,32,128]{4,3,1,0,2:T(8,128)(2,1)} %get-tuple-element.32) | copy-start | bytes 3932164
  956.1 219.6 %all-gather.11.cloned.1.call-start = ((), (), s32[]{:S(2)}) async-start(), calls=%async_computation.12 | async-start | bytes 19660800 | tf_op jit(solution)/shard_map/all_gather | solution.py:66
  1074.2 224.1 %reduce-scatter.9.cloned.1.call-start = ((), (), s32[]{:S(2)}) async-start(), calls=%async_computation.14 | async-start | bytes 19660800 | tf_op jit(solution)/shard_map/reduce_scatter | solution.py:246
  1074.3 18.8 copy-start.36
  1189.5 347.2 %all-to-all-start.1 = ((bf16[4,8,160,1536]{3,2,0,1:T(8,128)(2,1)}), bf16[4,8,160,1536]{3,2,0,1:T(8,128)(2,1)}, u32[]{:S(2)}, u32[]{:S(2)}) async-start(bf16[4,8,160,1536]{3,2,0,1:T(8,128)(2,1)} %copy.114), calls=%async_computation.3 | async-start | bytes 31457280 | tf_op jit(solution)/shard_map/all_to_all | solution.py:74
  1195.7 204.3 %all-gather.15.cloned.1.call-start = ((), (), s32[]{:S(2)}) async-start(), calls=%async_computation.15 | async-start | bytes 19660800 | tf_op jit(solution)/shard_map/all_gather | solution.py:66
  1413.2 129.4 %copy-start.77 = (f32[128]{0:T(128)S(1)}, f32[128]{0:T(128)}, u32[]{:S(2)}) copy-start(f32[128]{0:T(128)} %copy-done.76) | copy-start | bytes 1540
  1536.7 345.9 %all-to-all-start.3 = ((bf16[4,8,160,1536]{3,2,0,1:T(8,128)(2,1)}), bf16[4,8,160,1536]{3,2,0,1:T(8,128)(2,1)}, u32[]{:S(2)}, u32[]{:S(2)}) async-start(bf16[4,8,160,1536]{3,2,0,1:T(8,128)(2,1)} %copy.119), calls=%async_computation.6 | async-start | bytes 31457280 | tf_op jit(solution)/shard_map/all_to_all | solution.py:74
  1542.4 481.4 %all-gather.17.cloned.1.call-start = ((), (), s32[]{:S(2)}) async-start(), calls=%async_computation.16 | async-start | bytes 1966080 | tf_op jit(solution)/shard_map/all_gather | solution.py:264
  1542.6 347.2 %copy-start.2 = (s32[1024,1]{0,1:T(1,128)S(1)}, s32[1024,1]{0,1:T(1,128)}, u32[]{:S(2)}) copy-start(s32[1024,1]{0,1:T(1,128)} %get-tuple-element.44) | copy-start | bytes 12292
  1913.1 23.2 copy-start.53
  1913.1 23.2 copy-start.83
  1936.3 8.4 copy-start.9
  1936.3 8.4 copy-start.19
  1947.2 5.3 copy-start.15
  1949.3 76.9 %copy-start.12 = (f32[128,1536]{1,0:T(8,128)}, f32[128,1536]{1,0:T(8,128)S(1)}, u32[]{:S(2)}) copy-start(f32[128,1536]{1,0:T(8,128)S(1)} %get-tuple-element.54) | copy-start | bytes 2359300
  1949.3 74.5 %copy-start.41 = (bf16[384,1536]{1,0:T(8,128)(2,1)S(1)}, bf16[384,1536]{1,0:T(8,128)(2,1)}, u32[]{:S(2)}) copy-start(bf16[384,1536]{1,0:T(8,128)(2,1)} %param.20) | copy-start | bytes 3538948
  1951.7 106.1 %all-reduce.10.cloned.1.call-start = ((), (), s32[]{:S(2)}) async-start(), calls=%async_computation.18 | async-start | bytes 491520 | tf_op jit(solution)/shard_map/psum | solution.py:324
  1954.3 71.9 %copy-start.17 = (pred[512,512]{0,1:T(8,128)(4,1)S(1)}, pred[512,512]{0,1:T(8,128)(4,1)}, u32[]{:S(2)}) copy-start(pred[512,512]{0,1:T(8,128)(4,1)} %copy-done.16) | copy-start | bytes 786436
  1954.3 136.5 %reduce-scatter.11.cloned.1.call-start = ((), (), s32[]{:S(2)}) async-start(), calls=%async_computation.17 | async-start | bytes 1966080 | tf_op jit(solution)/shard_map/reduce_scatter | solution.py:314
  2023.8 6.5 slice-start
  2026.2 4.1 slice-start.1
  2026.2 4.1 copy-start.55
  2040.6 278.0 %all-reduce.12.cloned.1.call-start = ((), (), s32[]{:S(2)}) async-start(), calls=%async_computation.19 | async-start | bytes 13074432 | tf_op jit(solution)/shard_map/psum | solution.py:320
  2059.1 9.8 copy-start.39
  2068.9 10.9 copy-start.37
  2079.9 10.9 copy-start.11
  2079.9 10.9 copy-start.66
  2079.9 10.9 copy-start.81
  2079.9 12.3 copy-start.71
  2079.9 62.7 %copy-start.88 = (f32[128]{0:T(128)S(1)}, f32[128]{0:T(128)}, u32[]{:S(2)}) copy-start(f32[128]{0:T(128)} %copy-done.87) | copy-start | bytes 1540
  2079.9 62.7 %copy-start.8 = (f32[128,1536]{1,0:T(8,128)S(1)}, f32[128,1536]{1,0:T(8,128)}, u32[]{:S(2)}) copy-start(f32[128,1536]{1,0:T(8,128)} %copy-done.6) | copy-start | bytes 2359300
  2079.9 62.7 %copy-start.13 = (f32[128,1536]{1,0:T(8,128)S(1)}, f32[128,1536]{1,0:T(8,128)}, u32[]{:S(2)}) copy-start(f32[128,1536]{1,0:T(8,128)} %copy-done.12) | copy-start | bytes 2359300
  2079.9 62.7 %copy-start.20 = (bf16[128,1536]{1,0:T(8,128)(2,1)S(1)}, bf16[128,1536]{1,0:T(8,128)(2,1)}, u32[]{:S(2)}) copy-start(bf16[128,1536]{1,0:T(8,128)(2,1)} %param.26) | copy-start | bytes 1179652
  2079.9 62.7 %copy-start.24 = (f32[128,1536]{1,0:T(8,128)S(1)}, f32[128,1536]{1,0:T(8,128)}, u32[]{:S(2)}) copy-start(f32[128,1536]{1,0:T(8,128)} %get-tuple-element.17) | copy-start | bytes 2359300
  2079.9 62.7 %copy-start.85 = (f32[128]{0:T(128)S(1)}, f32[128]{0:T(128)}, u32[]{:S(2)}) copy-start(f32[128]{0:T(128)} %copy-done.84) | copy-start | bytes 1540
  2318.6 4.3 copy-start.44
  2318.6 5.1 copy-start.25
  2322.0 3.9 copy-start.1
  (46 other events, 86.6 us)
Sparse Core Ops, SparseCore 0:
  11.7 22.3 all-gather.6
  48.5 37.9 reduce-scatter.4
  104.8 99.9 all-gather.12
  231.7 100.3 all-gather.8
  956.2 117.9 reduce-scatter.6
  1075.7 99.9 all-gather.10
  1178.5 119.8 reduce-scatter.8
  1300.0 99.9 all-gather.14
  1951.8 71.9 all-gather.16
  2026.7 31.0 all-reduce.9
  2060.3 28.8 reduce-scatter.10
  2095.2 223.3 all-reduce.11
